TPU v7x, 128 devices: a whole 4x4x4 slice. The times are simulated.
128 devices in a mesh: row: 16 (over y_lo, x, core), col: 8 (over z, y_hi).
Axes of the slice: x: 4, y: 4 (y_hi: 2, y_lo: 2; y = y_hi * 2 + y_lo), z: 4, core: 2. Of those that a mesh axis runs over, the one named last changes fastest.
Arguments:
- positions: float32 [3, 131072], P(None, ('row', 'col')), may hold values from 0 to 1
- segments: float32 [3, 131072], P(None, ('row', 'col')), may hold values from -1.2 to 1.2
- radius: float32 [131072], P(('row', 'col')), may hold values from 0.05 to 0.2
- currents: float32 [2, 131072], P(None, ('row', 'col')), may hold values from -6 to 6
- resist: float32 [131072], P(('row', 'col')), may hold values from 0.3 to 3
- slot_of: int32 [131072], P(('row', 'col')), may hold values from 0 to 1023, as said below
- pair_list: int32 [4096, 2], P(('row', 'col')), may hold values from 0 to 255, as said below
- near_flag: int32 [4096], P(('row', 'col')), may hold values from 0 to 2, as said below
Outputs:
- voltage: float32 [2, 131072], P(None, ('row', 'col'))
Inputs may be any that keep to these rules, and one draw needn't show every extreme that they name: `slot_of`: the elements of shard d hold the values 0 to 1023 once each; a value s puts the element in cluster d * 2 + s // 512. `pair_list`: shard d = r * 8 + c lists 32 slots; each live slot holds a pair (I, J) with I <= J, I in clusters r * 2 * 8 to (r + 1) * 2 * 8 - 1 and (J // 2) % 8 = c; a pair stands in one live slot at most, over all shards. Empty slots hold I = r * 2 * 8 and J = c * 2. `near_flag`: 0 marks an empty slot.
All inputs are finite; a program needn't handle non-finite values.
Results may differ from a plain program's by a relative error of at most 0.0003.
Values sent between devices are 32-bit elements; how exact they have to be, the bound alone decides.
No kernel may reach another device: no remote copies, remote signals or barrier semaphores. Data moves between devices by JAX's collectives and lax.ppermute only.
A program may use at most 64 MiB of HBM per device.

v0:
```python
import math

import jax
import jax.numpy as jnp
from jax import lax
from jax.sharding import PartitionSpec as P

CS = 512


gauss_step = 0.5 / math.sqrt(3.0)
kernel_gain = 0.25
group_size = 4


def copy_for_each(value, axis):
    copies = jnp.broadcast_to(value, (lax.axis_size(axis), *value.shape))
    return lax.all_to_all(copies, axis, split_axis=0, concat_axis=0, tiled=True)


def in_order(blocks, dim):
    shape = list(blocks.shape[1:])
    shape[dim] *= blocks.shape[0]
    return jnp.moveaxis(blocks, 0, dim).reshape(shape)


def collect(value, axis, dim):
    blocks = copy_for_each(value, axis)
    return in_order(blocks, dim)


def cut_along(value, dim, peers):
    shape = value.shape
    blocks = value.reshape(*shape[:dim], peers, shape[dim] // peers, *shape[dim + 1 :])
    return jnp.moveaxis(blocks, dim, 0)


def sent_and_summed(value, axis, dim):
    peers = lax.axis_size(axis)
    blocks = lax.all_to_all(cut_along(value, dim, peers), axis, 0, 0, tiled=True)
    return jnp.sum(blocks, axis=0)


def tile_block(
    points_first, vectors_first, radii_first, points_second, vectors_second, radii_second, is_near
):
    softening = radii_first[:, None] ** 2 + radii_second[None, :] ** 2
    alignment = vectors_first[0][:, None] * vectors_second[0][None, :]
    for component in (1, 2):
        alignment = (
            alignment + vectors_first[component][:, None] * vectors_second[component][None, :]
        )

    def far_part():
        squared = softening
        for component in range(3):
            squared = (
                squared
                + (points_first[component][:, None] - points_second[component][None, :]) ** 2
            )
        return 1.0 / jnp.sqrt(squared)

    def near_part():
        summed = jnp.zeros_like(softening)
        for sign_first in (-1.0, 1.0):
            for sign_second in (-1.0, 1.0):
                squared = softening
                for component in range(3):
                    moved_first = (
                        points_first[component] + sign_first * gauss_step * vectors_first[component]
                    )
                    moved_second = (
                        points_second[component]
                        + sign_second * gauss_step * vectors_second[component]
                    )
                    squared = squared + (moved_first[:, None] - moved_second[None, :]) ** 2
                summed = summed + 1.0 / jnp.sqrt(squared)
        return 0.25 * summed

    inverse = lax.cond(is_near, near_part, far_part)
    return kernel_gain * alignment * inverse


def slot_terms(block_first, block_second, flag_value, diagonal_pair):
    step_rows = min(128, CS)

    def live_terms():
        is_near = flag_value == 2
        rows_out = []
        mirror_sum = jnp.zeros((2, CS), jnp.float32)
        for offset in range(0, CS, step_rows):
            portion = block_first[:, offset : offset + step_rows]
            kernel_tile = tile_block(
                portion[0:3],
                portion[3:6],
                portion[6],
                block_second[0:3],
                block_second[3:6],
                block_second[6],
                is_near,
            )
            rows_out.append(
                jnp.dot(block_second[7:9], kernel_tile.T, precision=lax.Precision.HIGHEST)
            )
            mirror_sum = mirror_sum + jnp.dot(
                portion[7:9], kernel_tile, precision=lax.Precision.HIGHEST
            )
        mirror_weight = 1.0 - diagonal_pair.astype(jnp.float32)
        return (jnp.concatenate(rows_out, 1), mirror_weight * mirror_sum)

    def empty_terms():
        blank = jnp.zeros((2, CS), jnp.float32)
        return (blank, blank)

    return lax.cond(flag_value > 0, live_terms, empty_terms)


def on_device(positions, segments, radius, currents, resist, slot_of, pair_list, near_flag):
    local_count = positions.shape[1]
    packed = jnp.concatenate([positions, segments, radius[None, :], currents], 0)
    ordered = jnp.zeros_like(packed).at[:, slot_of].set(packed)
    row_block = collect(ordered, "col", 1)
    col_block = collect(ordered, "row", 1)
    col_count = lax.axis_size("col")
    row_count = lax.axis_size("row")
    row_pos = lax.axis_index("row")
    per_device = local_count // CS
    row_span = per_device * col_count
    col_span = per_device * row_count
    slot_count = pair_list.shape[0]
    local_first = pair_list[:, 0] - row_pos * row_span
    local_second = pair_list[:, 1] // row_span * per_device + pair_list[:, 1] % per_device
    diagonal_all = (pair_list[:, 0] == pair_list[:, 1]).astype(jnp.int32)

    def add_terms(sums_pair, slot_index, direct_part, mirror_part):
        row_sum, col_sum = sums_pair
        first_id = local_first[slot_index]
        second_id = local_second[slot_index]
        current = lax.dynamic_slice_in_dim(row_sum, first_id * CS, CS, 1)
        row_sum = lax.dynamic_update_slice_in_dim(row_sum, current + direct_part, first_id * CS, 1)
        current = lax.dynamic_slice_in_dim(col_sum, second_id * CS, CS, 1)
        col_sum = lax.dynamic_update_slice_in_dim(col_sum, current + mirror_part, second_id * CS, 1)
        return (row_sum, col_sum)

    row_start = jnp.zeros((2, row_span * CS), jnp.float32)
    col_start = jnp.zeros((2, col_span * CS), jnp.float32)

    def visit_group(group_index, sums_now):
        for inner in range(group_size):
            slot_index = group_index * group_size + inner
            block_first = lax.dynamic_slice_in_dim(row_block, local_first[slot_index] * CS, CS, 1)
            block_second = lax.dynamic_slice_in_dim(col_block, local_second[slot_index] * CS, CS, 1)
            direct_part, mirror_part = slot_terms(
                block_first, block_second, near_flag[slot_index], diagonal_all[slot_index] > 0
            )
            sums_now = add_terms(sums_now, slot_index, direct_part, mirror_part)
        return sums_now

    row_sum, col_sum = lax.fori_loop(
        0, slot_count // group_size, visit_group, (row_start, col_start)
    )
    owned = sent_and_summed(row_sum, "col", 1) + sent_and_summed(col_sum, "row", 1)
    induced = owned[:, slot_of]
    voltage_real = resist * currents[0] - induced[1]
    voltage_imag = resist * currents[1] + induced[0]
    return jnp.stack([voltage_real, voltage_imag])


def solution(mesh):
    return jax.shard_map(
        on_device,
        mesh=mesh,
        in_specs=(
            P(None, ("row", "col")),
            P(None, ("row", "col")),
            P(("row", "col")),
            P(None, ("row", "col")),
            P(("row", "col")),
            P(("row", "col")),
            P(("row", "col"), None),
            P(("row", "col")),
        ),
        out_specs=P(None, ("row", "col")),
        check_vma=False,
    )
```

profile of v0, /device:TPU:1, one launch (start us, length us, event | category | flops | bytes accessed | tf_op | source)
XLA Modules:
  0.0 418.6 jit_solution(1951678659949175005)
XLA Ops:
  5.2 19.0 %all_to_all.20 = f32[8,9,1024]{2,1,0:T(8,128)S(1)} all-to-all(f32[8,9,1024]{2,1,0:T(8,128)S(1)} %broadcast_in_dim.20), channel_id=1, replica_groups=mesh['row'=16,'col'=8] {'col'}, dimensions={0} | all-to-all | bytes 589824 | tf_op jit(solution)/shard_map/all_to_all | solution.py:18
  25.2 6.3 %all-to-all-start = ((f32[16,9,1024]{2,1,0:T(8,128)}), f32[16,9,1024]{2,1,0:T(8,128)S(1)}, u32[]{:S(2)}, u32[]{:S(2)}) async-start(f32[16,9,1024]{2,1,0:T(8,128)} %broadcast_in_dim.19), calls=%async_computation | async-start | bytes 2097152 | tf_op jit(solution)/shard_map/all_to_all | solution.py:18
  32.8 14.6 %all-to-all-done = f32[16,9,1024]{2,1,0:T(8,128)S(1)} async-done(((f32[16,9,1024]{2,1,0:T(8,128)}), f32[16,9,1024]{2,1,0:T(8,128)S(1)}, u32[]{:S(2)}, u32[]{:S(2)}) %all-to-all-start) | async-done | bytes 589856 | tf_op jit(solution)/shard_map/all_to_all | solution.py:18
  49.2 288.0 %while.17 = (s32[]{:T(128)}, f32[2,8192]{1,0:T(2,128)S(1)}, f32[2,16384]{1,0:T(2,128)}, s32[32]{0:T(128)S(1)}, s32[32]{0:T(128)S(1)}, /*index=5*/s32[32]{0:T(128...) while((s32[]{:T(128)}, f32[2,8192]{1,0:T(2,128)S(1)}, ...), condition=%wide.region_42.43_spmd, body=%wide.region_1.42_spmd.sunk | while | flops 108167248 | bytes 22747132 | solution.py:159
  53.2 6.6 %conditional.24 = (f32[2,512]{1,0:T(2,128)S(1)}, f32[2,512]{1,0:T(2,128)S(1)}) conditional(s32[]{:T(128)} %convert_element_type.97, () %tuple.535, (f32[9,16384]{1,0:T(8,128)S(1)}, s32[]{:T(128)}, f32[9,8192]{1,0:T(8,128)S(1)}, s32[]{:T(128)}, s32[]{:T(128)}, /*index=5*/s32[32]{0:T(128)S(1)}, s32[]{:T(128)}) %tuple.536), branch_computations={%region_2.2_spmd, %region_3.11_spmd} | conditional | flops 27039756 | bytes 5661272 | solution.py:115
  67.1 6.6 %conditional.27 = (f32[2,512]{1,0:T(2,128)S(1)}, f32[2,512]{1,0:T(2,128)S(1)}) conditional(s32[]{:T(128)} %convert_element_type.100, () %tuple.541, (f32[9,16384]{1,0:T(8,128)S(1)}, s32[]{:T(128)}, f32[9,8192]{1,0:T(8,128)S(1)}, s32[]{:T(128)}, s32[]{:T(128)}, /*index=5*/s32[32]{0:T(128)S(1)}, s32[]{:T(128)}) %tuple.542), branch_computations={%region_32.32_spmd, %region_33.41_spmd} | conditional | flops 27039756 | bytes 5661272 | solution.py:115
  81.5 6.6 %conditional.24 = (f32[2,512]{1,0:T(2,128)S(1)}, f32[2,512]{1,0:T(2,128)S(1)}) conditional(s32[]{:T(128)} %convert_element_type.97, () %tuple.535, (f32[9,16384]{1,0:T(8,128)S(1)}, s32[]{:T(128)}, f32[9,8192]{1,0:T(8,128)S(1)}, s32[]{:T(128)}, s32[]{:T(128)}, /*index=5*/s32[32]{0:T(128)S(1)}, s32[]{:T(128)}) %tuple.536), branch_computations={%region_2.2_spmd, %region_3.11_spmd} | conditional | flops 27039756 | bytes 5661272 | solution.py:115
  91.4 6.8 %conditional.25 = (f32[2,512]{1,0:T(2,128)S(1)}, f32[2,512]{1,0:T(2,128)S(1)}) conditional(s32[]{:T(128)} %convert_element_type.98, () %tuple.537, (f32[9,16384]{1,0:T(8,128)S(1)}, s32[]{:T(128)}, f32[9,8192]{1,0:T(8,128)S(1)}, s32[]{:T(128)}, s32[]{:T(128)}, /*index=5*/s32[32]{0:T(128)S(1)}, s32[]{:T(128)}) %tuple.538), branch_computations={%region_12.12_spmd, %region_13.21_spmd} | conditional | flops 27039756 | bytes 5661272 | solution.py:115
  102.1 6.6 %conditional.27 = (f32[2,512]{1,0:T(2,128)S(1)}, f32[2,512]{1,0:T(2,128)S(1)}) conditional(s32[]{:T(128)} %convert_element_type.100, () %tuple.541, (f32[9,16384]{1,0:T(8,128)S(1)}, s32[]{:T(128)}, f32[9,8192]{1,0:T(8,128)S(1)}, s32[]{:T(128)}, s32[]{:T(128)}, /*index=5*/s32[32]{0:T(128)S(1)}, s32[]{:T(128)}) %tuple.542), branch_computations={%region_32.32_spmd, %region_33.41_spmd} | conditional | flops 27039756 | bytes 5661272 | solution.py:115
  116.6 6.6 %conditional.24 = (f32[2,512]{1,0:T(2,128)S(1)}, f32[2,512]{1,0:T(2,128)S(1)}) conditional(s32[]{:T(128)} %convert_element_type.97, () %tuple.535, (f32[9,16384]{1,0:T(8,128)S(1)}, s32[]{:T(128)}, f32[9,8192]{1,0:T(8,128)S(1)}, s32[]{:T(128)}, s32[]{:T(128)}, /*index=5*/s32[32]{0:T(128)S(1)}, s32[]{:T(128)}) %tuple.536), branch_computations={%region_2.2_spmd, %region_3.11_spmd} | conditional | flops 27039756 | bytes 5661272 | solution.py:115
  128.5 6.7 %conditional.26 = (f32[2,512]{1,0:T(2,128)S(1)}, f32[2,512]{1,0:T(2,128)S(1)}) conditional(s32[]{:T(128)} %convert_element_type.99, () %tuple.539, (f32[9,16384]{1,0:T(8,128)S(1)}, s32[]{:T(128)}, f32[9,8192]{1,0:T(8,128)S(1)}, s32[]{:T(128)}, s32[]{:T(128)}, /*index=5*/s32[32]{0:T(128)S(1)}, s32[]{:T(128)}) %tuple.540), branch_computations={%region_22.22_spmd, %region_23.31_spmd} | conditional | flops 27039756 | bytes 5661272 | solution.py:115
  137.0 6.6 %conditional.27 = (f32[2,512]{1,0:T(2,128)S(1)}, f32[2,512]{1,0:T(2,128)S(1)}) conditional(s32[]{:T(128)} %convert_element_type.100, () %tuple.541, (f32[9,16384]{1,0:T(8,128)S(1)}, s32[]{:T(128)}, f32[9,8192]{1,0:T(8,128)S(1)}, s32[]{:T(128)}, s32[]{:T(128)}, /*index=5*/s32[32]{0:T(128)S(1)}, s32[]{:T(128)}) %tuple.542), branch_computations={%region_32.32_spmd, %region_33.41_spmd} | conditional | flops 27039756 | bytes 5661272 | solution.py:115
  151.4 7.9 %conditional.24 = (f32[2,512]{1,0:T(2,128)S(1)}, f32[2,512]{1,0:T(2,128)S(1)}) conditional(s32[]{:T(128)} %convert_element_type.97, () %tuple.535, (f32[9,16384]{1,0:T(8,128)S(1)}, s32[]{:T(128)}, f32[9,8192]{1,0:T(8,128)S(1)}, s32[]{:T(128)}, s32[]{:T(128)}, /*index=5*/s32[32]{0:T(128)S(1)}, s32[]{:T(128)}) %tuple.536), branch_computations={%region_2.2_spmd, %region_3.11_spmd} | conditional | flops 27039756 | bytes 5661272 | solution.py:115
  162.7 6.8 %conditional.25 = (f32[2,512]{1,0:T(2,128)S(1)}, f32[2,512]{1,0:T(2,128)S(1)}) conditional(s32[]{:T(128)} %convert_element_type.98, () %tuple.537, (f32[9,16384]{1,0:T(8,128)S(1)}, s32[]{:T(128)}, f32[9,8192]{1,0:T(8,128)S(1)}, s32[]{:T(128)}, s32[]{:T(128)}, /*index=5*/s32[32]{0:T(128)S(1)}, s32[]{:T(128)}) %tuple.538), branch_computations={%region_12.12_spmd, %region_13.21_spmd} | conditional | flops 27039756 | bytes 5661272 | solution.py:115
  171.4 6.7 %conditional.26 = (f32[2,512]{1,0:T(2,128)S(1)}, f32[2,512]{1,0:T(2,128)S(1)}) conditional(s32[]{:T(128)} %convert_element_type.99, () %tuple.539, (f32[9,16384]{1,0:T(8,128)S(1)}, s32[]{:T(128)}, f32[9,8192]{1,0:T(8,128)S(1)}, s32[]{:T(128)}, s32[]{:T(128)}, /*index=5*/s32[32]{0:T(128)S(1)}, s32[]{:T(128)}) %tuple.540), branch_computations={%region_22.22_spmd, %region_23.31_spmd} | conditional | flops 27039756 | bytes 5661272 | solution.py:115
  179.9 6.6 %conditional.27 = (f32[2,512]{1,0:T(2,128)S(1)}, f32[2,512]{1,0:T(2,128)S(1)}) conditional(s32[]{:T(128)} %convert_element_type.100, () %tuple.541, (f32[9,16384]{1,0:T(8,128)S(1)}, s32[]{:T(128)}, f32[9,8192]{1,0:T(8,128)S(1)}, s32[]{:T(128)}, s32[]{:T(128)}, /*index=5*/s32[32]{0:T(128)S(1)}, s32[]{:T(128)}) %tuple.542), branch_computations={%region_32.32_spmd, %region_33.41_spmd} | conditional | flops 27039756 | bytes 5661272 | solution.py:115
  194.4 6.6 %conditional.24 = (f32[2,512]{1,0:T(2,128)S(1)}, f32[2,512]{1,0:T(2,128)S(1)}) conditional(s32[]{:T(128)} %convert_element_type.97, () %tuple.535, (f32[9,16384]{1,0:T(8,128)S(1)}, s32[]{:T(128)}, f32[9,8192]{1,0:T(8,128)S(1)}, s32[]{:T(128)}, s32[]{:T(128)}, /*index=5*/s32[32]{0:T(128)S(1)}, s32[]{:T(128)}) %tuple.536), branch_computations={%region_2.2_spmd, %region_3.11_spmd} | conditional | flops 27039756 | bytes 5661272 | solution.py:115
  204.3 6.8 %conditional.25 = (f32[2,512]{1,0:T(2,128)S(1)}, f32[2,512]{1,0:T(2,128)S(1)}) conditional(s32[]{:T(128)} %convert_element_type.98, () %tuple.537, (f32[9,16384]{1,0:T(8,128)S(1)}, s32[]{:T(128)}, f32[9,8192]{1,0:T(8,128)S(1)}, s32[]{:T(128)}, s32[]{:T(128)}, /*index=5*/s32[32]{0:T(128)S(1)}, s32[]{:T(128)}) %tuple.538), branch_computations={%region_12.12_spmd, %region_13.21_spmd} | conditional | flops 27039756 | bytes 5661272 | solution.py:115
  213.0 6.7 %conditional.26 = (f32[2,512]{1,0:T(2,128)S(1)}, f32[2,512]{1,0:T(2,128)S(1)}) conditional(s32[]{:T(128)} %convert_element_type.99, () %tuple.539, (f32[9,16384]{1,0:T(8,128)S(1)}, s32[]{:T(128)}, f32[9,8192]{1,0:T(8,128)S(1)}, s32[]{:T(128)}, s32[]{:T(128)}, /*index=5*/s32[32]{0:T(128)S(1)}, s32[]{:T(128)}) %tuple.540), branch_computations={%region_22.22_spmd, %region_23.31_spmd} | conditional | flops 27039756 | bytes 5661272 | solution.py:115
  229.5 6.6 %conditional.24 = (f32[2,512]{1,0:T(2,128)S(1)}, f32[2,512]{1,0:T(2,128)S(1)}) conditional(s32[]{:T(128)} %convert_element_type.97, () %tuple.535, (f32[9,16384]{1,0:T(8,128)S(1)}, s32[]{:T(128)}, f32[9,8192]{1,0:T(8,128)S(1)}, s32[]{:T(128)}, s32[]{:T(128)}, /*index=5*/s32[32]{0:T(128)S(1)}, s32[]{:T(128)}) %tuple.536), branch_computations={%region_2.2_spmd, %region_3.11_spmd} | conditional | flops 27039756 | bytes 5661272 | solution.py:115
  239.4 6.8 %conditional.25 = (f32[2,512]{1,0:T(2,128)S(1)}, f32[2,512]{1,0:T(2,128)S(1)}) conditional(s32[]{:T(128)} %convert_element_type.98, () %tuple.537, (f32[9,16384]{1,0:T(8,128)S(1)}, s32[]{:T(128)}, f32[9,8192]{1,0:T(8,128)S(1)}, s32[]{:T(128)}, s32[]{:T(128)}, /*index=5*/s32[32]{0:T(128)S(1)}, s32[]{:T(128)}) %tuple.538), branch_computations={%region_12.12_spmd, %region_13.21_spmd} | conditional | flops 27039756 | bytes 5661272 | solution.py:115
  248.1 6.7 %conditional.26 = (f32[2,512]{1,0:T(2,128)S(1)}, f32[2,512]{1,0:T(2,128)S(1)}) conditional(s32[]{:T(128)} %convert_element_type.99, () %tuple.539, (f32[9,16384]{1,0:T(8,128)S(1)}, s32[]{:T(128)}, f32[9,8192]{1,0:T(8,128)S(1)}, s32[]{:T(128)}, s32[]{:T(128)}, /*index=5*/s32[32]{0:T(128)S(1)}, s32[]{:T(128)}) %tuple.540), branch_computations={%region_22.22_spmd, %region_23.31_spmd} | conditional | flops 27039756 | bytes 5661272 | solution.py:115
  264.6 6.6 %conditional.24 = (f32[2,512]{1,0:T(2,128)S(1)}, f32[2,512]{1,0:T(2,128)S(1)}) conditional(s32[]{:T(128)} %convert_element_type.97, () %tuple.535, (f32[9,16384]{1,0:T(8,128)S(1)}, s32[]{:T(128)}, f32[9,8192]{1,0:T(8,128)S(1)}, s32[]{:T(128)}, s32[]{:T(128)}, /*index=5*/s32[32]{0:T(128)S(1)}, s32[]{:T(128)}) %tuple.536), branch_computations={%region_2.2_spmd, %region_3.11_spmd} | conditional | flops 27039756 | bytes 5661272 | solution.py:115
  274.4 6.8 %conditional.25 = (f32[2,512]{1,0:T(2,128)S(1)}, f32[2,512]{1,0:T(2,128)S(1)}) conditional(s32[]{:T(128)} %convert_element_type.98, () %tuple.537, (f32[9,16384]{1,0:T(8,128)S(1)}, s32[]{:T(128)}, f32[9,8192]{1,0:T(8,128)S(1)}, s32[]{:T(128)}, s32[]{:T(128)}, /*index=5*/s32[32]{0:T(128)S(1)}, s32[]{:T(128)}) %tuple.538), branch_computations={%region_12.12_spmd, %region_13.21_spmd} | conditional | flops 27039756 | bytes 5661272 | solution.py:115
  283.2 6.7 %conditional.26 = (f32[2,512]{1,0:T(2,128)S(1)}, f32[2,512]{1,0:T(2,128)S(1)}) conditional(s32[]{:T(128)} %convert_element_type.99, () %tuple.539, (f32[9,16384]{1,0:T(8,128)S(1)}, s32[]{:T(128)}, f32[9,8192]{1,0:T(8,128)S(1)}, s32[]{:T(128)}, s32[]{:T(128)}, /*index=5*/s32[32]{0:T(128)S(1)}, s32[]{:T(128)}) %tuple.540), branch_computations={%region_22.22_spmd, %region_23.31_spmd} | conditional | flops 27039756 | bytes 5661272 | solution.py:115
  291.7 6.6 %conditional.27 = (f32[2,512]{1,0:T(2,128)S(1)}, f32[2,512]{1,0:T(2,128)S(1)}) conditional(s32[]{:T(128)} %convert_element_type.100, () %tuple.541, (f32[9,16384]{1,0:T(8,128)S(1)}, s32[]{:T(128)}, f32[9,8192]{1,0:T(8,128)S(1)}, s32[]{:T(128)}, s32[]{:T(128)}, /*index=5*/s32[32]{0:T(128)S(1)}, s32[]{:T(128)}) %tuple.542), branch_computations={%region_32.32_spmd, %region_33.41_spmd} | conditional | flops 27039756 | bytes 5661272 | solution.py:115
  306.2 6.6 %conditional.24 = (f32[2,512]{1,0:T(2,128)S(1)}, f32[2,512]{1,0:T(2,128)S(1)}) conditional(s32[]{:T(128)} %convert_element_type.97, () %tuple.535, (f32[9,16384]{1,0:T(8,128)S(1)}, s32[]{:T(128)}, f32[9,8192]{1,0:T(8,128)S(1)}, s32[]{:T(128)}, s32[]{:T(128)}, /*index=5*/s32[32]{0:T(128)S(1)}, s32[]{:T(128)}) %tuple.536), branch_computations={%region_2.2_spmd, %region_3.11_spmd} | conditional | flops 27039756 | bytes 5661272 | solution.py:115
  316.1 6.8 %conditional.25 = (f32[2,512]{1,0:T(2,128)S(1)}, f32[2,512]{1,0:T(2,128)S(1)}) conditional(s32[]{:T(128)} %convert_element_type.98, () %tuple.537, (f32[9,16384]{1,0:T(8,128)S(1)}, s32[]{:T(128)}, f32[9,8192]{1,0:T(8,128)S(1)}, s32[]{:T(128)}, s32[]{:T(128)}, /*index=5*/s32[32]{0:T(128)S(1)}, s32[]{:T(128)}) %tuple.538), branch_computations={%region_12.12_spmd, %region_13.21_spmd} | conditional | flops 27039756 | bytes 5661272 | solution.py:115
  326.8 6.6 %conditional.27 = (f32[2,512]{1,0:T(2,128)S(1)}, f32[2,512]{1,0:T(2,128)S(1)}) conditional(s32[]{:T(128)} %convert_element_type.100, () %tuple.541, (f32[9,16384]{1,0:T(8,128)S(1)}, s32[]{:T(128)}, f32[9,8192]{1,0:T(8,128)S(1)}, s32[]{:T(128)}, s32[]{:T(128)}, /*index=5*/s32[32]{0:T(128)S(1)}, s32[]{:T(128)}) %tuple.542), branch_computations={%region_32.32_spmd, %region_33.41_spmd} | conditional | flops 27039756 | bytes 5661272 | solution.py:115
  337.2 45.0 %all_to_all.21 = f32[8,2,1024]{2,1,0:T(2,128)S(1)} all-to-all(f32[8,2,1024]{2,1,0:T(2,128)S(1)} %bitcast.660), channel_id=1, replica_groups=mesh['row'=16,'col'=8] {'col'}, dimensions={0} | all-to-all | bytes 131072 | tf_op jit(solution)/shard_map/all_to_all | solution.py:40
  382.2 25.3 %all-to-all-start.3 = ((f32[16,2,1024]{2,1,0:T(2,128)}), f32[16,2,1024]{2,1,0:T(2,128)S(1)}, u32[]{:S(2)}, u32[]{:S(2)}) async-start(f32[16,2,1024]{2,1,0:T(2,128)} %bitcast.394), calls=%async_computation.3 | async-start | bytes 262144 | tf_op jit(solution)/shard_map/all_to_all | solution.py:40
  407.5 6.1 %all-to-all-done.3 = f32[16,2,1024]{2,1,0:T(2,128)S(1)} async-done(((f32[16,2,1024]{2,1,0:T(2,128)}), f32[16,2,1024]{2,1,0:T(2,128)S(1)}, u32[]{:S(2)}, u32[]{:S(2)}) %all-to-all-start.3) | async-done | bytes 131104 | tf_op jit(solution)/shard_map/all_to_all | solution.py:40
  (937 shorter events, 226.8 us)
Async XLA Ops:
  0.0 0.7 copy-start.1
  0.0 0.7 copy-start.2
  25.2 22.1 %all-to-all-start = ((f32[16,9,1024]{2,1,0:T(8,128)}), f32[16,9,1024]{2,1,0:T(8,128)S(1)}, u32[]{:S(2)}, u32[]{:S(2)}) async-start(f32[16,9,1024]{2,1,0:T(8,128)} %broadcast_in_dim.19), calls=%async_computation | async-start | bytes 2097152 | tf_op jit(solution)/shard_map/all_to_all | solution.py:18
  31.5 0.7 copy-start.4
  48.5 0.7 copy-start
  382.2 31.5 %all-to-all-start.3 = ((f32[16,2,1024]{2,1,0:T(2,128)}), f32[16,2,1024]{2,1,0:T(2,128)S(1)}, u32[]{:S(2)}, u32[]{:S(2)}) async-start(f32[16,2,1024]{2,1,0:T(2,128)} %bitcast.394), calls=%async_computation.3 | async-start | bytes 262144 | tf_op jit(solution)/shard_map/all_to_all | solution.py:40
  417.3 0.7 copy-start.3
where the time goes:
time: 422 us; the launch traced here: 419 us
  loops' own time  101 us (24%)
  matrix products  75.6 us (18%)
  other arithmetic  70.2 us (17%)
  blocking collectives  63.9 us (15%)
  local copies, waits for them, and re-layouts  55.3 us (13%)
  starting transfers between devices  31.6 us (7%)
  waiting for transfers between devices  20.7 us (5%)
    another operation x1, loops' own time, on_device(): lax.fori_loop(0, slot_count // group_size, visit_group, (row_start, col_s...  63.2 us
    all_to_all x1, blocking collectives, sent_and_summed(): lax.all_to_all(cut_along(value, dim, peers), axis, 0, 0, tiled=True)  45 us
    dynamic_update_slice x32, other arithmetic, add_terms(): lax.dynamic_update_slice_in_dim(col_sum, current + mirror_part, second_id...  40.7 us
    dot_general x100, matrix products, live_terms(): jnp.dot(block_second[7:9], kernel_tile.T, precision=lax.Precision.HIGHEST)  38.4 us
    dot_general x100, matrix products, live_terms(): jnp.dot(portion[7:9], kernel_tile, precision=lax.Precision.HIGHEST)  37.2 us
    another operation x32, loops' own time, slot_terms(): return lax.cond(flag_value > 0, live_terms, empty_terms)  35.7 us
    all_to_all x1, starting transfers between devices, sent_and_summed(): lax.all_to_all(cut_along(value, dim, peers), axis, 0, 0, tiled=True)  25.3 us
    all_to_all x1, blocking collectives, copy_for_each(): return lax.all_to_all(copies, axis, split_axis=0, concat_axis=0, tiled=True)  19 us
  transfers between devices with their start and end apart: 2, of which 2 were waited for; matrix products, arithmetic and copies ran while one was open for 0% of the time, Pallas kernels for 0%

commit v1 on v0

v1 whole, which is shorter than its diff:
```python
import math
import jax
import jax.numpy as jnp
from jax import lax
from jax.experimental import pallas as pl
from jax.experimental.pallas import tpu as pltpu
from jax.sharding import PartitionSpec as P_

CS = 512
G = 0.5 / math.sqrt(3.0)
f32, bf16 = jnp.float32, jnp.bfloat16
M = 128
TN = (((0,), (0,)), ((), ()))
NT = (((1,), (1,)), ((), ()))


def split3(x):
    a = x.astype(bf16).astype(f32)
    r = x - a
    b = r.astype(bf16).astype(f32)
    return a, b, r - b


def rows8():
    return lax.broadcasted_iota(jnp.int32, (8, CS), 0)


def moved(P, L, s):
    if s == 0:
        return P, P[3:4]
    w = (G * L) * (2.0 * s * P + G * L)
    n = P[3:4] + ((w[0:1] + w[1:2]) + w[2:3])
    return P + (s * G) * L, n


def dist_tiles(P, L, s, first):
    Q, n = moved(P, L, s)
    r = rows8()
    if first:
        t = jnp.where(r < 3, -2.0 * Q, jnp.where(r == 3, n, jnp.where(r == 4, 1.0, 0.0)))
    else:
        t = jnp.where(r < 3, Q, jnp.where(r == 3, 1.0, jnp.where(r == 4, n, 0.0)))
    a, b, c = split3(t)
    low = jnp.where(r < 5, 0.0, 1.0)
    if first:
        one = r == 4
        b = jnp.where(one, 1.0, b)
        c = jnp.where(one, 1.0, c)
        a5, b5 = pltpu.roll(a, 5, 0), pltpu.roll(b, 5, 0)
        return [jnp.where(r < 5, a, a5), jnp.where(r < 5, b, a5), jnp.where(r < 5, c, b5)]
    a5, b5, c5 = pltpu.roll(a, 5, 0), pltpu.roll(b, 5, 0), pltpu.roll(c, 5, 0)
    top = r < 4
    return [jnp.where(r < 5, a, b5),
            jnp.where(top, a, jnp.where(r == 4, b, c5)),
            jnp.where(top, a, jnp.where(r == 4, c, b5))]


def dot_tiles(L, scale, first):
    r = rows8()
    t = jnp.where(r < 3, L * scale, 0.0)
    a, b, _ = split3(t)
    a4, b4 = pltpu.roll(a, 4, 0), pltpu.roll(b, 4, 0)
    if first:
        return [a + a4, b + b4]
    return [a + b4, a + b4]


def load(ref, idx):
    dev = idx // 2
    h = idx % 2
    P = ref[dev, :, pl.ds(pl.multiple_of(h * CS, CS), CS)]
    ci = ref[dev, :, 1024:1152]
    ci = jnp.where(h == 1, pltpu.roll(ci, 4, 0), ci)
    return P, jnp.concatenate([ci[t:t + 1] for t in range(4)], 1)


def kernel(first_s, second_s, kind_s, row_ref, col_ref, ro_ref, co_ref, lt, cb, accd, accm, rhs):
    accm[...] = jnp.zeros_like(accm)
    zt = jnp.zeros((8, CS), f32)

    def prep(I, _):
        P, ci = load(row_ref, I)
        L = pltpu.roll(P, 4, 0)
        tiles = (dist_tiles(P, L, 0, True) + dist_tiles(P, L, 1.0, True)
                 + dist_tiles(P, L, -1.0, True) + dot_tiles(L, 0.25, True))
        r = rows8()
        cur = jnp.where(r == 0, P[7:8], jnp.where(r == 1, ci, 0.0))
        a, b, c = split3(cur)
        tiles += [a, b, c, zt, zt]
        full = jnp.concatenate(tiles, 0)
        T = full.T.astype(bf16)
        lt[I] = T
        sel = lax.broadcasted_iota(jnp.int32, (128, 256), 0)
        ln = lax.broadcasted_iota(jnp.int32, (128, 256), 1)
        ones = jnp.where((sel >= 88) & (sel < 112) & (sel % 8 == ln // 128), 1.0, 0.0).astype(bf16)
        o = jnp.dot(T, ones, preferred_element_type=f32)
        cb[I] = o
        accd[I] = jnp.zeros((CS, 256), f32)
        return 0

    lax.fori_loop(0, 16, prep, 0)

    def slot(k, _):
        I = first_s[k]
        J = second_s[k]
        kind = kind_s[k]

        def work(near):
            P, ci = load(col_ref, J)
            cr = P[7:8]
            L = pltpu.roll(P, 4, 0)
            if near:
                vp = dist_tiles(P, L, 1.0, False)
                vm = dist_tiles(P, L, -1.0, False)
                z3 = [zt] * 3
                mats = [z3 + vp + z3, z3 + vm + z3, z3 + z3 + vp, z3 + z3 + vm]
                mats = [m + [zt] * 7 for m in mats]
                mats += [[zt] * 9 + dot_tiles(L, 0.25, False) + [zt] * 5]
            else:
                mats = [dist_tiles(P, L, 0, False) + [zt] * 13,
                        [zt] * 9 + dot_tiles(L, 1.0, False) + [zt] * 5]
            R = [jnp.concatenate(m, 0).astype(bf16) for m in mats]
            mr = [[None] * 4, [None] * 4]
            crs = [jnp.broadcast_to(cr[:, 128 * t:128 * t + 128], (8, 128)) for t in range(4)]
            cis = [jnp.broadcast_to(ci[:, 128 * t:128 * t + 128], (8, 128)) for t in range(4)]
            for m in range(0, CS, M):
                lhs = lt[I, m:m + M, :]
                o = [jnp.dot(lhs, x, preferred_element_type=f32) for x in R]
                for q in range(0, M, 8):
                    bc = cb[I, m + q:m + q + 8, :]
                    br, bi = bc[:, :128], bc[:, 128:]
                    dr = di = None
                    for t in range(4):
                        ri = None
                        for x in o[:-1]:
                            v = lax.rsqrt(x[q:q + 8, 128 * t:128 * t + 128])
                            ri = v if ri is None else ri + v
                        g = ri * o[-1][q:q + 8, 128 * t:128 * t + 128]
                        a, b = g * crs[t], g * cis[t]
                        dr = a if dr is None else dr + a
                        di = b if di is None else di + b
                        a, b = g * br, g * bi
                        mr[0][t] = a if mr[0][t] is None else mr[0][t] + a
                        mr[1][t] = b if mr[1][t] is None else mr[1][t] + b
                    accd[I, m + q:m + q + 8, 0:128] += dr
                    accd[I, m + q:m + q + 8, 128:256] += di
            w = jnp.where(kind >= 4, 0.0, 1.0)
            for c in range(2):
                accm[J, c] += w * jnp.concatenate(mr[c], 1)

        @pl.when((kind & 3) == 1)
        def _():
            work(False)

        @pl.when((kind & 3) == 2)
        def _():
            work(True)
        return 0

    lax.fori_loop(0, 32, slot, 0)

    def fin_row(i, _):
        for h in range(2):
            x = accd[2 * i + h]
            hi = x.astype(bf16)
            lo = (x - hi.astype(f32)).astype(bf16)
            one = jnp.ones((8, 128), bf16)
            for c in range(2):
                s = lax.dot_general(one, hi[:, 128 * c:128 * c + 128], NT, preferred_element_type=f32)
                s = s + lax.dot_general(one, lo[:, 128 * c:128 * c + 128], NT, preferred_element_type=f32)
                ro_ref[i, c:c + 1, h * CS:(h + 1) * CS] = s[0:1]
        return 0
    lax.fori_loop(0, 8, fin_row, 0)

    def fin_col(i, _):
        for h in range(2):
            for c in range(2):
                co_ref[i, c:c + 1, h * CS:(h + 1) * CS] = jnp.sum(accm[2 * i + h, c], 0, keepdims=True)
        return 0
    lax.fori_loop(0, 16, fin_col, 0)


def pre_kernel(pos_ref, seg_ref, rad_ref, cur_ref, slot_ref, out_ref):
    q = pos_ref[...] - 0.5
    a = rad_ref[...]
    n = (q[0:1] * q[0:1] + q[1:2] * q[1:2]) + (q[2:3] * q[2:3] + a * a)
    A = jnp.concatenate([q, n, seg_ref[...], cur_ref[0:1]], 0)
    B = cur_ref[1:2]
    a0, a1, a2 = split3(A)
    b0, b1, b2 = split3(B)
    X = jnp.concatenate([a0, a1, a2, b0, b1, b2, jnp.zeros((5, 1024), f32)], 0).astype(bf16)
    S = jnp.broadcast_to(slot_ref[...].astype(f32), (128, 1024)).T
    lane = lax.broadcasted_iota(jnp.int32, (1024, 128), 1).astype(f32)
    for g in range(0, 8, 2):
        hot = jnp.concatenate([jnp.where(S == lane + 128.0 * (g + i), 1.0, 0.0) for i in range(2)], 1)
        o = jnp.dot(X, hot.astype(bf16), preferred_element_type=f32)
        out_ref[:, 128 * g:128 * g + 256] = o[0:8] + o[8:16] + o[16:24]
        b = o[24:25] + o[25:26] + o[26:27]
        out_ref[g:g + 1, 1024:1152] = b[:, 0:128]
        out_ref[g + 1:g + 2, 1024:1152] = b[:, 128:256]


def post_kernel(a_ref, b_ref, slot_ref, res_ref, cur_ref, out_ref):
    s = a_ref[0]
    for i in range(1, 8):
        s = s + a_ref[i]
    for i in range(16):
        s = s + b_ref[i]
    p = jnp.concatenate([*split3(s), jnp.zeros((10, 1024), f32)], 0).astype(bf16)
    row = lax.broadcasted_iota(jnp.int32, (1024, 256), 0)
    for g in range(4):
        e = slice(256 * g, 256 * g + 256)
        hot = jnp.where(row == slot_ref[:, e], 1.0, 0.0).astype(bf16)
        o = jnp.dot(p, hot, preferred_element_type=f32)
        o = o[0:2] + o[2:4] + o[4:6]
        r = res_ref[:, e]
        out_ref[0:1, e] = r * cur_ref[0:1, e] - o[1:2]
        out_ref[1:2, e] = r * cur_ref[1:2, e] + o[0:1]


def spread(value, axis):
    copies = jnp.broadcast_to(value, (lax.axis_size(axis), *value.shape))
    return lax.all_to_all(copies, axis, 0, 0, tiled=True)


SM = pl.BlockSpec(memory_space=pltpu.SMEM)
VM = pl.BlockSpec(memory_space=pltpu.VMEM)
PARAMS = pltpu.CompilerParams(vmem_limit_bytes=48 << 20)


def on_device(positions, segments, radius, currents, resist, slot_of, pair_list, near_flag):
    slot = slot_of.reshape(1, 1024)
    block = pl.pallas_call(
        pre_kernel, out_shape=jax.ShapeDtypeStruct((8, 1152), f32),
        in_specs=[VM] * 5, out_specs=VM, compiler_params=PARAMS, name="pre",
    )(positions, segments, radius.reshape(1, 1024), currents, slot)
    row = spread(block, "col")
    col = spread(block, "row")
    first = pair_list[:, 0] % 16
    second = pair_list[:, 1] // 16 * 2 + pair_list[:, 1] % 2
    kind = near_flag + jnp.where(pair_list[:, 0] == pair_list[:, 1], 4, 0)
    ro, co = pl.pallas_call(
        kernel,
        out_shape=(jax.ShapeDtypeStruct((8, 2, 1024), f32), jax.ShapeDtypeStruct((16, 2, 1024), f32)),
        in_specs=[SM, SM, SM, VM, VM], out_specs=(VM, VM),
        scratch_shapes=[pltpu.VMEM((16, CS, 128), bf16), pltpu.VMEM((16, CS, 256), f32),
                        pltpu.VMEM((16, CS, 256), f32), pltpu.VMEM((32, 2, 8, CS), f32),
                        pltpu.VMEM((8, 128), f32)],
        compiler_params=PARAMS, name="pairs",
    )(first, second, kind, row, col)
    a = lax.all_to_all(ro, "col", 0, 0, tiled=True)
    b = lax.all_to_all(co, "row", 0, 0, tiled=True)
    return pl.pallas_call(
        post_kernel, out_shape=jax.ShapeDtypeStruct((2, 1024), f32),
        in_specs=[VM] * 5, out_specs=VM, compiler_params=PARAMS, name="post",
    )(a, b, slot, resist.reshape(1, 1024), currents)


def solution(mesh):
    both = ("row", "col")
    return jax.shard_map(
        on_device, mesh=mesh,
        in_specs=(P_(None, both), P_(None, both), P_(both), P_(None, both), P_(both), P_(both),
                  P_(both, None), P_(both)),
        out_specs=P_(None, both), check_vma=False,
    )
```

time: 422 us -> 91.7 us (0.22)
  loops' own time: 101 us -> 0 us
  matrix products: 75.6 us -> 0 us
  other arithmetic: 70.2 us -> 0.01 us
  local copies, waits for them, and re-layouts: 55.3 us -> 4.4 us
  Pallas kernels: 0 us -> 27.8 us
  starting transfers between devices: 31.6 us -> 6.8 us
  blocking collectives: 63.9 us -> 41.1 us
  waiting for transfers between devices: 20.7 us -> 10.6 us
    another operation x133 -> x0, loops' own time: 101 us -> none  [the longest x1 63.2 us: on_device(): lax.fori_loop(0, slot_count // group_size, visit_group, (row_start, col_s...]
    dot_general x200 -> x0, matrix products: 75.6 us -> none  [the longest x100 38.4 us: live_terms(): jnp.dot(block_second[7:9], kernel_tile.T, precision=lax.Precision.HIGHEST)]
    dynamic_update_slice x56 -> x0, other arithmetic: 41 us -> none  [the longest x32 40.7 us: add_terms(): lax.dynamic_update_slice_in_dim(col_sum, current + mirror_part, second_id...]
    dynamic_slice x74 -> x0, local copies, waits for them, and re-layouts: 34 us -> none  [the longest x25 15.8 us: visit_group(): diagonal_all[slot_index] > 0]
    pallas_call x0 -> x3, Pallas kernels: none -> 27.8 us  [the longest x1 26.1 us: on_device(): pl.pallas_call(kernel, out_shape=(jax.ShapeDtypeStruct((8, 2, 1024), f32)...]
    all_to_all x2 -> x1, starting transfers between devices: 31.6 us -> 6.8 us  [spread(): return lax.all_to_all(copies, axis, 0, 0, tiled=True)]
    all_to_all x2 -> x3, blocking collectives: 63.9 us -> 41.1 us  [the longest x1 16.3 us: spread(): return lax.all_to_all(copies, axis, 0, 0, tiled=True)]
    sqrt x96 -> x0, other arithmetic: 15.8 us -> none  [far_part(): return 1.0 / jnp.sqrt(squared)]
  transfers between devices with their start and end apart: 2 -> 1, of which waited for: 2 -> 1; matrix products, arithmetic and copies ran while one was open for 0% -> 0% of each run, Pallas kernels for 0% -> 0%
where the time goes in v1:
time: 91.7 us; the launch traced here: 90.7 us
  blocking collectives  41.1 us (45%)
  Pallas kernels  27.8 us (30%)
  waiting for transfers between devices  10.6 us (12%)
  starting transfers between devices  6.8 us (7%)
  local copies, waits for them, and re-layouts  4.4 us (5%)
    pallas_call x1, Pallas kernels, on_device(): pl.pallas_call(kernel, out_shape=(jax.ShapeDtypeStruct((8, 2, 1024), f32)...  26.1 us
    all_to_all x1, blocking collectives, spread(): return lax.all_to_all(copies, axis, 0, 0, tiled=True)  16.3 us
    all_to_all x1, blocking collectives, on_device(): b = lax.all_to_all(co, 'row', 0, 0, tiled=True)  13 us
    all_to_all x1, blocking collectives, on_device(): a = lax.all_to_all(ro, 'col', 0, 0, tiled=True)  11.8 us
    all_to_all x1, waiting for transfers between devices, spread(): return lax.all_to_all(copies, axis, 0, 0, tiled=True)  10.6 us
    all_to_all x1, starting transfers between devices, spread(): return lax.all_to_all(copies, axis, 0, 0, tiled=True)  6.8 us
    unnamed x20, local copies, waits for them, and re-layouts  3.52 us
  transfers between devices with their start and end apart: 1, of which 1 were waited for; matrix products, arithmetic and copies ran while one was open for 0% of the time, Pallas kernels for 0%

profile of v1, /device:TPU:1, one launch (start us, length us, event | category | flops | bytes accessed | tf_op | source)
XLA Modules:
  0.0 90.7 jit_solution(14821744851609431559)
XLA Ops:
  0.0 0.0 copy-start
  0.0 0.7 copy-done
  0.7 0.0 copy-start.2
  0.7 0.7 copy-done.2
  1.4 0.0 copy-start.4
  1.4 0.7 copy-done.4
  2.1 0.0 copy-start.5
  2.1 0.7 copy-done.5
  2.8 0.0 copy-start.7
  2.8 0.7 copy-done.7
  3.5 0.6 pre.1
  4.1 16.3 %all_to_all.20.row_ref = f32[8,8,1152]{2,1,0:T(8,128)S(1)} all-to-all(f32[8,8,1152]{2,1,0:T(8,128)S(1)} %broadcast_in_dim.10), channel_id=1, replica_groups=mesh['row'=16,'col'=8] {'col'}, dimensions={0} | all-to-all | bytes 589824 | tf_op jit(solution)/shard_map/all_to_all | solution.py:223
  20.4 0.9 broadcast_in_dim.11
  21.3 0.0 copy-start.8
  21.3 0.0 copy-start.9
  21.3 6.8 %all-to-all-start.1 = ((f32[16,8,1152]{2,1,0:T(8,128)}), f32[16,8,1152]{2,1,0:T(8,128)S(1)}, u32[]{:S(2)}, u32[]{:S(2)}) async-start(f32[16,8,1152]{2,1,0:T(8,128)} %broadcast_in_dim.11), calls=%async_computation.1 | async-start | bytes 1179648 | tf_op jit(solution)/shard_map/all_to_all | solution.py:223
  28.1 0.0 copy-done.8
  28.1 0.0 copy-done.9
  28.1 10.6 %all-to-all-done.1.col_ref = f32[16,8,1152]{2,1,0:T(8,128)S(1)} async-done(((f32[16,8,1152]{2,1,0:T(8,128)}), f32[16,8,1152]{2,1,0:T(8,128)S(1)}, u32[]{:S(2)}, u32[]{:S(2)}) %all-to-all-start.1) | async-done | bytes 589856 | tf_op jit(solution)/shard_map/all_to_all | solution.py:223
  38.7 26.1 %pairs.1 = (f32[8,2,1024]{2,1,0:T(2,128)S(1)}, f32[16,2,1024]{2,1,0:T(2,128)S(1)}) custom-call(s32[32]{0:T(128)S(1)} %get-tuple-element.11.first_s, s32[32]{0:T(128)S(1)} %get-tuple-element.10.second_s, s32[32]{0:T(128)S(1)} %get-tuple-element.9.kind_s, f32[8,8,1152]{2,1,0:T(8,128)S(1)} %all_to_all.20.row_ref, f32[16,8,1152]{2,1,0:T(8,128)S(1)} %all-to-all-done.1.col_ref), custom_call_target="tpu_custom_call" | custom-call | tf_op jit(solution)/shard_map/pairs/pallas_call | solution.py:242
  64.8 11.8 %all_to_all.21.a_ref = f32[8,2,1024]{2,1,0:T(2,128)S(1)} all-to-all(f32[8,2,1024]{2,1,0:T(2,128)S(1)} %get-tuple-element.7), channel_id=1, replica_groups=mesh['row'=16,'col'=8] {'col'}, dimensions={0} | all-to-all | bytes 131072 | tf_op jit(solution)/shard_map/all_to_all | solution.py:251
  76.6 0.0 copy-start.1
  76.6 0.0 copy-start.3
  76.6 0.0 copy-start.6
  76.6 13.0 %all_to_all.22.b_ref = f32[16,2,1024]{2,1,0:T(2,128)S(1)} all-to-all(f32[16,2,1024]{2,1,0:T(2,128)S(1)} %get-tuple-element.8), channel_id=1, replica_groups=mesh['row'=16,'col'=8] {'row'}, dimensions={0} | all-to-all | bytes 262144 | tf_op jit(solution)/shard_map/all_to_all | solution.py:252
  89.6 0.0 copy-done.1
  89.6 0.0 copy-done.3
  89.6 0.0 copy-done.6
  89.6 1.1 %post.1 = f32[2,1024]{1,0:T(2,128)} custom-call(f32[8,2,1024]{2,1,0:T(2,128)S(1)} %all_to_all.21.a_ref, f32[16,2,1024]{2,1,0:T(2,128)S(1)} %all_to_all.22.b_ref, s32[1,1024]{1,0:T(1,128)S(1)} %bitcast.19, f32[1,1024]{1,0:T(1,128)S(1)} %bitcast.20, f32[2,1024]{1,0:T(2,128)S(1)} %copy-done.1), custom_call_target="tpu_custom_call" | custom-call | tf_op jit(solution)/shard_map/post/pallas_call | solution.py:253
  (2 shorter events, 0.0 us)
Async XLA Ops:
  0.0 0.7 copy-start
  0.7 0.7 copy-start.2
  1.4 0.7 copy-start.4
  2.1 0.7 copy-start.5
  2.8 0.7 copy-start.7
  21.3 6.8 %copy-start.8 = (s32[32,2]{0,1:T(2,128)S(1)}, s32[32,2]{0,1:T(2,128)}, u32[]{:S(2)}) copy-start(s32[32,2]{0,1:T(2,128)} %param.14) | copy-start | bytes 772
  21.3 6.8 %copy-start.9 = (s32[32]{0:T(128)S(1)}, s32[32]{0:T(128)}, u32[]{:S(2)}) copy-start(s32[32]{0:T(128)} %param.15) | copy-start | bytes 388
  21.3 17.4 %all-to-all-start.1 = ((f32[16,8,1152]{2,1,0:T(8,128)}), f32[16,8,1152]{2,1,0:T(8,128)S(1)}, u32[]{:S(2)}, u32[]{:S(2)}) async-start(f32[16,8,1152]{2,1,0:T(8,128)} %broadcast_in_dim.11), calls=%async_computation.1 | async-start | bytes 1179648 | tf_op jit(solution)/shard_map/all_to_all | solution.py:223
  76.6 13.0 %copy-start.1 = (f32[2,1024]{1,0:T(2,128)S(1)}, f32[2,1024]{1,0:T(2,128)}, u32[]{:S(2)}) copy-start(f32[2,1024]{1,0:T(2,128)} %cur_ref.3) | copy-start | bytes 24580
  76.6 13.0 %copy-start.3 = (s32[1024]{0:T(1024)S(1)}, s32[1024]{0:T(1024)}, u32[]{:S(2)}) copy-start(s32[1024]{0:T(1024)} %param.13) | copy-start | bytes 12292
  76.6 13.0 %copy-start.6 = (f32[1024]{0:T(1024)S(1)}, f32[1024]{0:T(1024)}, u32[]{:S(2)}) copy-start(f32[1024]{0:T(1024)} %param.12) | copy-start | bytes 12292

commit v2 on v1

v2 whole, which is shorter than its diff:
```python
import math
import jax
import jax.numpy as jnp
from jax import lax
from jax.experimental import pallas as pl
from jax.experimental.pallas import tpu as pltpu
from jax.sharding import PartitionSpec as P_

CS = 512
G = 0.5 / math.sqrt(3.0)
f32, bf16 = jnp.float32, jnp.bfloat16
M = 256
FAR_UNROLL = 2


def split3(x):
    a = x.astype(bf16).astype(f32)
    r = x - a
    b = r.astype(bf16).astype(f32)
    return a, b, r - b


def rows8():
    return lax.broadcasted_iota(jnp.int32, (8, CS), 0)


def moved(P, L, s):
    if s == 0:
        return P, P[3:4]
    w = (G * L) * (2.0 * s * P + G * L)
    n = P[3:4] + ((w[0:1] + w[1:2]) + w[2:3])
    return P + (s * G) * L, n


def dist_tiles(P, L, s, first):
    Q, n = moved(P, L, s)
    r = rows8()
    if first:
        t = jnp.where(r < 3, -2.0 * Q, jnp.where(r == 3, n, jnp.where(r == 4, 1.0, 0.0)))
    else:
        t = jnp.where(r < 3, Q, jnp.where(r == 3, 1.0, jnp.where(r == 4, n, 0.0)))
    a, b, c = split3(t)
    if first:
        b = jnp.where(r == 4, 1.0, b)
        c = jnp.where(r == 4, 1.0, c)
        a5, b5 = pltpu.roll(a, 5, 0), pltpu.roll(b, 5, 0)
        return [jnp.where(r < 5, a, a5), jnp.where(r < 5, b, a5), jnp.where(r < 5, c, b5)]
    a5, b5, c5 = pltpu.roll(a, 5, 0), pltpu.roll(b, 5, 0), pltpu.roll(c, 5, 0)
    return [jnp.where(r < 5, a, b5),
            jnp.where(r < 4, a, jnp.where(r == 4, b, c5)),
            jnp.where(r < 4, a, jnp.where(r == 4, c, b5))]


def dot_tiles(L, scale, first):
    t = jnp.where(rows8() < 3, L * scale, 0.0)
    a, b, c = split3(t)
    a4, b4, c4 = (pltpu.roll(x, 4, 0) for x in (a, b, c))
    if first:
        return [a + a4, b + b4, a + c4]
    return [a + b4, a + b4, c + a4]


def load(ref, idx):
    dev = idx // 2
    h = idx % 2
    P = ref[dev, :, pl.ds(pl.multiple_of(h * CS, CS), CS)]
    ci = ref[dev, :, 1024:1152]
    ci = jnp.where(h == 1, pltpu.roll(ci, 4, 0), ci)
    return P, jnp.concatenate([ci[t:t + 1] for t in range(4)], 1)


def prep_kernel(row_ref, lt):
    zt = jnp.zeros((8, CS), f32)

    def prep(I, _):
        P, ci = load(row_ref, I)
        L = pltpu.roll(P, 4, 0)
        r = rows8()
        cur = jnp.where(r == 0, P[7:8], jnp.where(r == 1, ci, 0.0))
        tiles = (dist_tiles(P, L, 0, True) + [zt] + dist_tiles(P, L, 1.0, True) + [zt]
                 + dist_tiles(P, L, -1.0, True) + [zt] + dot_tiles(L, 0.25, True) + [cur])
        lt[I] = jnp.concatenate(tiles, 0).T
        return 0

    lax.fori_loop(0, 16, prep, 0)


def kernel(pair_s, flag_s, lt_hbm, col_ref, r0, r1, r2, r3, c0, c1, c2, c3, accd, accm, far_s, near_s,
           lt, sem):
    fetch = pltpu.make_async_copy(lt_hbm, lt, sem)
    fetch.start()
    accm[...] = jnp.zeros_like(accm)
    zt = jnp.zeros((8, CS), f32)

    def clear(i, _):
        accd[i] = jnp.zeros((CS, 256), f32)
        return 0
    lax.fori_loop(0, 16, clear, 0)

    fetch.wait()
    me_row, me_col = pair_s[0, 0] // 16, pair_s[0, 1] // 2 % 8

    def sort(k, c):
        nf, nn = c
        I, J, fl = pair_s[k, 0], pair_s[k, 1], flag_s[k]
        code = (I % 16) ^ (2 * me_col)
        code = code + (J // 16 * 2 + J % 2) * 16 + 512
        code = jnp.where(I == J, code, code + 1024)
        far_s[nf] = code
        near_s[nn] = code
        return nf + (fl == 1).astype(jnp.int32), nn + (fl == 2).astype(jnp.int32)
    nf, nn = lax.fori_loop(0, 32, sort, (0, 0))
    for u in range(FAR_UNROLL):
        far_s[nf + u] = 0

    def open_pair(code, near):
        I, J = code % 16, code // 16 % 32
        wd = jnp.where((code // 512) % 2 == 1, 1.0, 0.0)
        wm = jnp.where(code // 1024 == 1, 1.0, 0.0)
        P, ci = load(col_ref, J)
        cr = P[7:8]
        L = pltpu.roll(P, 4, 0)
        z4 = [zt] * 4
        if near:
            vp = dist_tiles(P, L, 1.0, False) + [zt]
            vm = dist_tiles(P, L, -1.0, False) + [zt]
            mats = [z4 + vp + z4 + z4, z4 + z4 + vm + z4, z4 + vm + z4 + z4, z4 + z4 + vp + z4,
                    z4 * 3 + dot_tiles(L, 0.25, False) + [zt]]
            gain = 1.0
        else:
            mats = [dist_tiles(P, L, 0, False) + [zt] + z4 * 3,
                    z4 * 3 + dot_tiles(L, 1.0, False) + [zt]]
            gain = 1.0
        R = [jnp.concatenate(m, 0).astype(bf16) for m in mats]
        crs = [jnp.broadcast_to(cr[:, 128 * t:128 * t + 128] * (wd * gain), (8, 128)) for t in range(4)]
        cis = [jnp.broadcast_to(ci[:, 128 * t:128 * t + 128] * (wd * gain), (8, 128)) for t in range(4)]
        return dict(I=I, J=J, w=wm * gain, R=R, crs=crs, cis=cis, mr=[[None] * 4, [None] * 4])

    def advance(p, m, near):
        I, mr = p["I"], p["mr"]
        lhs = lt[I, m:m + M, :].astype(bf16)
        o = [jnp.dot(lhs, x, preferred_element_type=f32) for x in p["R"]]
        for q in range(0, M, 8):
            bc = lt[I, m + q:m + q + 8, :]
            br = jnp.broadcast_to(bc[:, 120:121], (8, 128))
            bi = jnp.broadcast_to(bc[:, 121:122], (8, 128))
            dr = di = None
            for t in range(4):
                x = [y[q:q + 8, 128 * t:128 * t + 128] for y in o]
                if near:
                    ri = (lax.rsqrt(x[0]) + lax.rsqrt(x[1])) + (lax.rsqrt(x[2]) + lax.rsqrt(x[3]))
                else:
                    ri = lax.rsqrt(x[0])
                g = ri * x[-1]
                a, b = g * p["crs"][t], g * p["cis"][t]
                dr = a if dr is None else dr + a
                di = b if di is None else di + b
                a, b = g * br, g * bi
                mr[0][t] = a if mr[0][t] is None else mr[0][t] + a
                mr[1][t] = b if mr[1][t] is None else mr[1][t] + b
            accd[I, m + q:m + q + 8, 0:128] += dr
            accd[I, m + q:m + q + 8, 128:256] += di

    def close_pair(p):
        for c in range(2):
            accm[p["J"], c] += p["w"] * jnp.concatenate(p["mr"][c], 1)

    def near_step(k, _):
        p = open_pair(near_s[k], True)
        for m in range(0, CS, M):
            advance(p, m, True)
        close_pair(p)
        return 0
    lax.fori_loop(0, nn, near_step, 0)

    def far_step(k, _):
        ps = [open_pair(far_s[FAR_UNROLL * k + u], False) for u in range(FAR_UNROLL)]
        for m in range(0, CS, M):
            for p in ps:
                advance(p, m, False)
        for p in ps:
            close_pair(p)
        return 0
    lax.fori_loop(0, (nf + FAR_UNROLL - 1) // FAR_UNROLL, far_step, 0)

    sel = lax.broadcasted_iota(jnp.int32, (256, 128), 0)
    ln = lax.broadcasted_iota(jnp.int32, (256, 128), 1)
    ones = jnp.where(sel // 128 == ln, 1.0, 0.0).astype(bf16)

    def fin_row(out, m):
        def step(i, _):
            for h in range(2):
                x = accd[4 * m + 2 * i + h]
                hi = x.astype(bf16)
                lo = (x - hi.astype(f32)).astype(bf16)
                s = (jnp.dot(hi, ones, preferred_element_type=f32)
                     + jnp.dot(lo, ones, preferred_element_type=f32))
                out[i, :, h * CS:(h + 1) * CS] = s.T[0:2]
            return 0
        lax.fori_loop(0, 2, step, 0)
    for m, out in enumerate((r0, r1, r2, r3)):
        fin_row(out, m)

    for m, out in enumerate((c0, c1, c2, c3)):
        for k in range(4):
            slot = k // 2 * 8 + 2 * m + k % 2
            src = 2 * jnp.bitwise_xor(slot, me_row)
            for h in range(2):
                for c in range(2):
                    out[k, c:c + 1, h * CS:(h + 1) * CS] = jnp.sum(accm[src + h, c], 0, keepdims=True)


SCRATCH = [pltpu.VMEM((16, CS, 256), f32), pltpu.VMEM((32, 2, 8, CS), f32),
           pltpu.SMEM((40,), jnp.int32), pltpu.SMEM((40,), jnp.int32),
           pltpu.VMEM((16, CS, 128), f32), pltpu.SemaphoreType.DMA]


def pre_kernel(pos_hbm, seg_hbm, rad_hbm, cur_hbm, slot_hbm, one_ref, all_ref,
               pos_ref, seg_ref, rad_ref, cur_ref, slot_ref, sems):
    moves = [pltpu.make_async_copy(a, b, sems.at[i]) for i, (a, b) in enumerate(
        ((pos_hbm, pos_ref), (seg_hbm, seg_ref), (rad_hbm, rad_ref), (cur_hbm, cur_ref),
         (slot_hbm, slot_ref)))]
    out_ref = one_ref.at[0]
    for move in moves:
        move.start()
    for move in moves:
        move.wait()
    q = pos_ref[...] - 0.5
    a = rad_ref[...]
    n = (q[0:1] * q[0:1] + q[1:2] * q[1:2]) + (q[2:3] * q[2:3] + a * a)
    A = jnp.concatenate([q, n, seg_ref[...], cur_ref[0:1]], 0)
    B = cur_ref[1:2]
    a0, a1, a2 = split3(A)
    b0, b1, b2 = split3(B)
    X = jnp.concatenate([a0, a1, a2, b0, b1, b2, jnp.zeros((5, 1024), f32)], 0).astype(bf16)
    S = jnp.broadcast_to(slot_ref[...].astype(f32), (128, 1024)).T
    lane = lax.broadcasted_iota(jnp.int32, (1024, 128), 1).astype(f32)
    for g in range(0, 8, 2):
        hot = jnp.concatenate([jnp.where(S == lane + 128.0 * (g + i), 1.0, 0.0) for i in range(2)], 1)
        o = jnp.dot(X, hot.astype(bf16), preferred_element_type=f32)
        out_ref[:, 128 * g:128 * g + 256] = o[0:8] + o[8:16] + o[16:24]
        b = o[24:25] + o[25:26] + o[26:27]
        out_ref[g:g + 1, 1024:1152] = b[:, 0:128]
        out_ref[g + 1:g + 2, 1024:1152] = b[:, 128:256]
    for i in range(16):
        all_ref[i] = out_ref[...]


def post_kernel(a_ref, b_ref, c_ref, d_ref, slot_ref, res_ref, cur_ref, out_ref):
    s = (a_ref[0] + b_ref[0]) + (c_ref[0] + d_ref[0])
    p = jnp.concatenate([*split3(s), jnp.zeros((10, 1024), f32)], 0).astype(bf16)
    row = lax.broadcasted_iota(jnp.int32, (1024, 256), 0)
    for g in range(4):
        e = slice(256 * g, 256 * g + 256)
        hot = jnp.where(row == slot_ref[:, e], 1.0, 0.0).astype(bf16)
        o = jnp.dot(p, hot, preferred_element_type=f32)
        o = o[0:2] + o[2:4] + o[4:6]
        r = res_ref[:, e]
        out_ref[0:1, e] = r * cur_ref[0:1, e] - o[1:2]
        out_ref[1:2, e] = r * cur_ref[1:2, e] + o[0:1]


SM = pl.BlockSpec(memory_space=pltpu.SMEM)
VM = pl.BlockSpec(memory_space=pltpu.VMEM)
HB = pl.BlockSpec(memory_space=pltpu.HBM)
BIG = pltpu.CompilerParams(vmem_limit_bytes=61 << 20)
PARAMS = pltpu.CompilerParams(vmem_limit_bytes=24 << 20)


def shape(*dims):
    return jax.ShapeDtypeStruct(dims, f32)


def swap(value, axis, k):
    return lax.ppermute(value, axis, [(i, i ^ k) for i in range(lax.axis_size(axis))])


def on_device(positions, segments, radius, currents, resist, slot_of, pair_list, near_flag):
    slot = slot_of.reshape(1, 1024)
    block, copies = pl.pallas_call(
        pre_kernel, out_shape=(shape(1, 8, 1152), shape(16, 8, 1152)),
        in_specs=[HB] * 5, out_specs=(VM, VM),
        scratch_shapes=[pltpu.VMEM((3, 1024), f32), pltpu.VMEM((3, 1024), f32),
                        pltpu.VMEM((1, 1024), f32), pltpu.VMEM((2, 1024), f32),
                        pltpu.VMEM((1, 1024), jnp.int32), pltpu.SemaphoreType.DMA((5,))],
        compiler_params=pltpu.CompilerParams(vmem_limit_bytes=62 << 20), name="pre",
    )(positions, segments, radius.reshape(1, 1024), currents, slot)
    col = lax.all_to_all(copies, "row", 0, 0, tiled=True)
    two = jnp.concatenate([block, swap(block, "col", 1)], 0)
    row = jnp.concatenate([two] + [swap(two, "col", 2 * m) for m in (1, 2, 3)], 0)
    lt = pl.pallas_call(
        prep_kernel, out_shape=shape(16, CS, 128), in_specs=[VM], out_specs=VM,
        compiler_params=BIG, name="prep",
        cost_estimate=pl.CostEstimate(flops=10**9, bytes_accessed=5 << 20, transcendentals=0),
    )(row)
    outs = pl.pallas_call(
        kernel, out_shape=(shape(2, 2, 1024),) * 4 + (shape(4, 2, 1024),) * 4,
        in_specs=[SM, SM, HB, VM], out_specs=(VM,) * 8, scratch_shapes=SCRATCH,
        compiler_params=BIG, name="pairs",
    )(pair_list, near_flag, lt, col)
    a, b = outs[:4], outs[4:]
    b = [b[0]] + [swap(b[m], "row", 2 * m) for m in (1, 2, 3)]
    a = [a[0]] + [swap(a[m], "col", 2 * m) for m in (1, 2, 3)]
    b = (b[0] + b[1]) + (b[2] + b[3])
    a = (a[0] + a[1]) + (a[2] + a[3])
    b = b[0:2] + swap(b[2:4], "row", 8)
    parts = (a[0:1], swap(a[1:2], "col", 1), b[0:1], swap(b[1:2], "row", 1))
    return pl.pallas_call(
        post_kernel, out_shape=shape(2, 1024), in_specs=[VM] * 7, out_specs=VM,
        compiler_params=PARAMS, name="post",
    )(*parts, slot, resist.reshape(1, 1024), currents)


def solution(mesh):
    both = ("row", "col")
    return jax.shard_map(
        on_device, mesh=mesh,
        in_specs=(P_(None, both), P_(None, both), P_(both), P_(None, both), P_(both), P_(both),
                  P_(both, None), P_(both)),
        out_specs=P_(None, both), check_vma=False,
    )
```

time: 91.7 us -> 81.4 us (0.89)
  blocking collectives: 41.1 us -> 0 us
  starting transfers between devices: 6.8 us -> 29.7 us
  Pallas kernels: 27.8 us -> 36.8 us
  waiting for transfers between devices: 10.6 us -> 9.04 us
  other arithmetic: 0.01 us -> 1.52 us
    all_to_all x3 -> x0, blocking collectives: 41.1 us -> none  [the longest x1 16.3 us: spread(): return lax.all_to_all(copies, axis, 0, 0, tiled=True)]
    ppermute x0 -> x13, starting transfers between devices: none -> 22.2 us  [swap(): lax.ppermute(value, axis, [(i, i ^ k) for i in range(lax.axis_size(axis))])]
    all_to_all x1, waiting for transfers between devices: 10.6 us -> 0.01 us  [on_device(): col = lax.all_to_all(copies, 'row', 0, 0, tiled=True)]
    ppermute x0 -> x13, waiting for transfers between devices: none -> 9.04 us  [swap(): lax.ppermute(value, axis, [(i, i ^ k) for i in range(lax.axis_size(axis))])]
    pallas_call x3 -> x4, Pallas kernels: 27.8 us -> 36.8 us  [the longest x1 28.2 us: on_device(): pl.pallas_call(kernel, out_shape=(shape(2, 2, 1024),) * 4 + (shape(4, 2,...]
    add x1 -> x3, other arithmetic: 0.01 us -> 1.52 us  [the longest x1 0.77 us: on_device(): b = b[0] + b[1] + (b[2] + b[3])]
    unnamed x20 -> x14, local copies, waits for them, and re-layouts: 3.52 us -> 3.73 us
  transfers between devices with their start and end apart: 1 -> 14, of which waited for: 1 -> 5; matrix products, arithmetic and copies ran while one was open for 0% -> 4% of each run, Pallas kernels for 0% -> 7%
where the time goes in v2:
time: 81.4 us; the launch traced here: 80.9 us
  Pallas kernels  36.8 us (45%)
  starting transfers between devices  29.7 us (36%)
  waiting for transfers between devices  9.04 us (11%)
  local copies, waits for them, and re-layouts  3.75 us (5%)
  other arithmetic  1.52 us (2%)
    pallas_call x1, Pallas kernels, on_device(): pl.pallas_call(kernel, out_shape=(shape(2, 2, 1024),) * 4 + (shape(4, 2,...  28.2 us
    ppermute x13, starting transfers between devices, swap(): lax.ppermute(value, axis, [(i, i ^ k) for i in range(lax.axis_size(axis))])  22.2 us
    ppermute x13, waiting for transfers between devices, swap(): lax.ppermute(value, axis, [(i, i ^ k) for i in range(lax.axis_size(axis))])  9.04 us
    all_to_all x1, starting transfers between devices, on_device(): col = lax.all_to_all(copies, 'row', 0, 0, tiled=True)  7.43 us
    pallas_call x1, Pallas kernels, on_device(): pl.pallas_call(prep_kernel, out_shape=shape(16, CS, 128), in_specs=[VM],...  5.29 us
    unnamed x14, local copies, waits for them, and re-layouts  3.73 us
    pallas_call x1, Pallas kernels, on_device(): pl.pallas_call(pre_kernel, out_shape=(shape(1, 8, 1152), shape(16, 8, 115...  2.23 us
  transfers between devices with their start and end apart: 14, of which 5 were waited for; matrix products, arithmetic and copies ran while one was open for 4% of the time, Pallas kernels for 7%

profile of v2, /device:TPU:1, one launch (start us, length us, event | category | flops | bytes accessed | tf_op | source)
XLA Modules:
  0.0 80.9 jit_solution(5396389946278093830)
XLA Ops:
  0.0 2.2 %pre.1 = (f32[1,8,1152]{2,1,0:T(8,128)}, f32[16,8,1152]{2,1,0:T(8,128)}) custom-call(f32[3,1024]{1,0:T(4,128)} %pos_hbm.1, f32[3,1024]{1,0:T(4,128)} %seg_hbm.1, f32[1,1024]{1,0:T(1,128)} %bitcast.17, f32[2,1024]{1,0:T(2,128)} %cur_ref.1, s32[1,1024]{1,0:T(1,128)} %bitcast.8), custom_call_target="tpu_custom_call" | custom-call | tf_op jit(solution)/shard_map/pre/pallas_call | solution.py:280
  2.2 3.8 %collective-permute-start = (f32[1,8,1152]{2,1,0:T(8,128)}, f32[1,8,1152]{2,1,0:T(8,128)S(1)}, u32[]{:S(2)}, u32[]{:S(2)}) collective-permute-start(f32[1,8,1152]{2,1,0:T(8,128)} %get-tuple-element.15), channel_id=1, source_target_pairs={{0,1},{1,0},{2,3},{3,2},{4,5},{5,4},{6,7},{7,6},{8,9},{9,8},{10,11... | collective-permute-start | bytes 110600 | tf_op jit(solution)/shard_map/ppermute | solution.py:275
  6.1 0.8 constant_dynamic-update-slice_fusion.1
  6.9 0.8 collective-permute-done
  7.6 1.7 %collective-permute-start.1 = (f32[2,8,1152]{2,1,0:T(8,128)S(1)}, f32[2,8,1152]{2,1,0:T(8,128)S(1)}, u32[]{:S(2)}, u32[]{:S(2)}) collective-permute-start(f32[2,8,1152]{2,1,0:T(8,128)S(1)} %get-tuple-element.25), channel_id=1, source_target_pairs={{0,2},{1,3},{2,0},{3,1},{4,6},{5,7},{6,4},{7,5},{8,10},{9,11},{10,... | collective-permute-start | bytes 221192 | tf_op jit(solution)/shard_map/ppermute | solution.py:275
  9.3 7.4 %all-to-all-start = ((f32[16,8,1152]{2,1,0:T(8,128)}), f32[16,8,1152]{2,1,0:T(8,128)S(1)}, u32[]{:S(2)}, u32[]{:S(2)}) async-start(f32[16,8,1152]{2,1,0:T(8,128)} %get-tuple-element.16), calls=%async_computation | async-start | bytes 1179648 | tf_op jit(solution)/shard_map/all_to_all | solution.py:288
  16.7 1.4 %copy.9.pair_s = s32[32,2]{1,0:T(8,128)} copy(s32[32,2]{0,1:T(2,128)} %param.14) | data formatting | bytes 512 | tf_op args[6]
  18.1 2.3 %collective-permute-start.3 = (f32[2,8,1152]{2,1,0:T(8,128)S(1)}, f32[2,8,1152]{2,1,0:T(8,128)S(1)}, u32[]{:S(2)}, u32[]{:S(2)}) collective-permute-start(f32[2,8,1152]{2,1,0:T(8,128)S(1)} %get-tuple-element.25), channel_id=1, source_target_pairs={{0,6},{1,7},{2,4},{3,5},{4,2},{5,3},{6,0},{7,1},{8,14},{9,15},{10,... | collective-permute-start | bytes 221192 | tf_op jit(solution)/shard_map/ppermute | solution.py:275
  20.4 1.1 %collective-permute-start.2 = (f32[2,8,1152]{2,1,0:T(8,128)S(1)}, f32[2,8,1152]{2,1,0:T(8,128)S(1)}, u32[]{:S(2)}, u32[]{:S(2)}) collective-permute-start(f32[2,8,1152]{2,1,0:T(8,128)S(1)} %get-tuple-element.25), channel_id=1, source_target_pairs={{0,4},{1,5},{2,6},{3,7},{4,0},{5,1},{6,2},{7,3},{8,12},{9,13},{10,... | collective-permute-start | bytes 221192 | tf_op jit(solution)/shard_map/ppermute | solution.py:275
  21.4 3.9 %collective-permute-done.2 = f32[2,8,1152]{2,1,0:T(8,128)S(1)} collective-permute-done((f32[2,8,1152]{2,1,0:T(8,128)S(1)}, f32[2,8,1152]{2,1,0:T(8,128)S(1)}, u32[]{:S(2)}, u32[]{:S(2)}) %collective-permute-start.2) | collective-permute-done | bytes 73760 | tf_op jit(solution)/shard_map/ppermute | solution.py:275
  25.4 0.7 copy-done.4
  26.1 5.3 %prep.1.lt_hbm = f32[16,512,128]{2,1,0:T(8,128)} custom-call(f32[8,8,1152]{2,1,0:T(8,128)} %copy-done.4), custom_call_target="tpu_custom_call" | custom-call | flops 1000000000 | bytes 5242880 | tf_op jit(solution)/shard_map/prep/pallas_call | solution.py:291
  31.4 0.8 %copy-done.3 = f32[16,8,1152]{2,1,0:T(8,128)} copy-done((f32[16,8,1152]{2,1,0:T(8,128)}, f32[16,8,1152]{2,1,0:T(8,128)S(1)}, u32[]{:S(2)}) %copy-start.3) | copy-done | bytes 589848
  32.3 28.2 %pairs.1 = (f32[2,2,1024]{2,1,0:T(2,128)}, f32[2,2,1024]{2,1,0:T(2,128)}, f32[2,2,1024]{2,1,0:T(2,128)}, f32[2,2,1024]{2,1,0:T(2,128)}, f32[4,2,1024]{2,1,0:T(2,...) custom-call(s32[32,2]{1,0:T(8,128)} %copy.9.pair_s, s32[32]{0:T(128)} %flag_s.1, ...), custom_call_target="tpu_custom_call" | custom-call | tf_op jit(solution)/shard_map/pairs/pallas_call | solution.py:296
  60.5 0.1 collective-permute-start.4
  60.5 0.1 collective-permute-start.5
  60.6 3.8 %collective-permute-start.6 = (f32[2,2,1024]{2,1,0:T(2,128)}, f32[2,2,1024]{2,1,0:T(2,128)S(1)}, u32[]{:S(2)}, u32[]{:S(2)}) collective-permute-start(f32[2,2,1024]{2,1,0:T(2,128)} %get-tuple-element.20), channel_id=1, source_target_pairs={{0,6},{1,7},{2,4},{3,5},{4,2},{5,3},{6,0},{7,1},{8,14},{9,15},{10,... | collective-permute-start | bytes 49160 | tf_op jit(solution)/shard_map/ppermute | solution.py:275
  64.4 0.0 collective-permute-start.8
  64.4 0.0 collective-permute-start.9
  64.4 0.0 collective-permute-done.4
  64.4 3.9 %collective-permute-start.10 = (f32[4,2,1024]{2,1,0:T(2,128)}, f32[4,2,1024]{2,1,0:T(2,128)S(1)}, u32[]{:S(2)}, u32[]{:S(2)}) collective-permute-start(f32[4,2,1024]{2,1,0:T(2,128)} %get-tuple-element.24), channel_id=1, source_target_pairs={{0,48},{8,56},{16,32},{24,40},{32,16},{40,24},{48,0},{56,8},{64,11... | collective-permute-start | bytes 98312 | tf_op jit(solution)/shard_map/ppermute | solution.py:275
  68.3 0.0 collective-permute-done.6
  68.3 0.7 add_add_fusion.1
  69.0 0.0 collective-permute-done.8
  69.0 0.7 collective-permute-done.10
  69.8 0.8 add_add_fusion
  70.6 0.1 collective-permute-start.11
  70.7 0.1 collective-permute-start.7
  70.8 2.8 %collective-permute-done.11 = f32[2,2,1024]{2,1,0:T(2,128)S(1)} collective-permute-done((f32[2,2,1024]{2,1,0:T(2,128)S(1)}, f32[2,2,1024]{2,1,0:T(2,128)S(1)}, u32[]{:S(2)}, u32[]{:S(2)}) %collective-permute-start.11) | collective-permute-done | bytes 16416 | tf_op jit(solution)/shard_map/ppermute | solution.py:275
  73.5 5.4 %collective-permute-start.12 = (f32[1,2,1024]{2,1,0:T(2,128)S(1)}, f32[1,2,1024]{2,1,0:T(2,128)S(1)}, u32[]{:S(2)}, u32[]{:S(2)}) collective-permute-start(f32[1,2,1024]{2,1,0:T(2,128)S(1)} %get-tuple-element.29), channel_id=1, source_target_pairs={{0,8},{8,0},{16,24},{24,16},{32,40},{40,32},{48,56},{56,48},{64,72... | collective-permute-start | bytes 24584 | tf_op jit(solution)/shard_map/ppermute | solution.py:275
  79.0 0.8 %collective-permute-done.12.d_ref = f32[1,2,1024]{2,1,0:T(2,128)S(1)} collective-permute-done((f32[1,2,1024]{2,1,0:T(2,128)S(1)}, f32[1,2,1024]{2,1,0:T(2,128)S(1)}, u32[]{:S(2)}, u32[]{:S(2)}) %collective-permute-start.12) | collective-permute-done | bytes 8224 | tf_op jit(solution)/shard_map/ppermute | solution.py:275
  79.8 1.1 %post.1 = f32[2,1024]{1,0:T(2,128)} custom-call(f32[1,2,1024]{2,1,0:T(2,128)S(1)} %get-tuple-element.32.a_ref, f32[1,2,1024]{2,1,0:T(2,128)S(1)} %collective-permute-done.7.b_ref, f32[1,2,1024]{2,1,0:T(2,128)S(1)} %get-tuple-element.30.c_ref, f32[1,2,1024]{2,1,0:T(2,128)S(1)} %collective-permute-done.12.d_ref, s32[1,1024]{1,0:T(1,128)S(1)} %bitcast.9, ...), custom_call_target="tpu_custom_call" | custom-call | tf_op jit(solution)/shard_map/post/pallas_call | solution.py:308
  (22 shorter events, 0.1 us)
Async XLA Ops:
  2.2 5.4 %collective-permute-start = (f32[1,8,1152]{2,1,0:T(8,128)}, f32[1,8,1152]{2,1,0:T(8,128)S(1)}, u32[]{:S(2)}, u32[]{:S(2)}) collective-permute-start(f32[1,8,1152]{2,1,0:T(8,128)} %get-tuple-element.15), channel_id=1, source_target_pairs={{0,1},{1,0},{2,3},{3,2},{4,5},{5,4},{6,7},{7,6},{8,9},{9,8},{10,11... | collective-permute-start | bytes 110600 | tf_op jit(solution)/shard_map/ppermute | solution.py:275
  7.6 13.8 %collective-permute-start.1 = (f32[2,8,1152]{2,1,0:T(8,128)S(1)}, f32[2,8,1152]{2,1,0:T(8,128)S(1)}, u32[]{:S(2)}, u32[]{:S(2)}) collective-permute-start(f32[2,8,1152]{2,1,0:T(8,128)S(1)} %get-tuple-element.25), channel_id=1, source_target_pairs={{0,2},{1,3},{2,0},{3,1},{4,6},{5,7},{6,4},{7,5},{8,10},{9,11},{10,... | collective-permute-start | bytes 221192 | tf_op jit(solution)/shard_map/ppermute | solution.py:275
  9.3 22.1 %all-to-all-start = ((f32[16,8,1152]{2,1,0:T(8,128)}), f32[16,8,1152]{2,1,0:T(8,128)S(1)}, u32[]{:S(2)}, u32[]{:S(2)}) async-start(f32[16,8,1152]{2,1,0:T(8,128)} %get-tuple-element.16), calls=%async_computation | async-start | bytes 1179648 | tf_op jit(solution)/shard_map/all_to_all | solution.py:288
  18.1 7.3 %collective-permute-start.3 = (f32[2,8,1152]{2,1,0:T(8,128)S(1)}, f32[2,8,1152]{2,1,0:T(8,128)S(1)}, u32[]{:S(2)}, u32[]{:S(2)}) collective-permute-start(f32[2,8,1152]{2,1,0:T(8,128)S(1)} %get-tuple-element.25), channel_id=1, source_target_pairs={{0,6},{1,7},{2,4},{3,5},{4,2},{5,3},{6,0},{7,1},{8,14},{9,15},{10,... | collective-permute-start | bytes 221192 | tf_op jit(solution)/shard_map/ppermute | solution.py:275
  20.4 5.0 %collective-permute-start.2 = (f32[2,8,1152]{2,1,0:T(8,128)S(1)}, f32[2,8,1152]{2,1,0:T(8,128)S(1)}, u32[]{:S(2)}, u32[]{:S(2)}) collective-permute-start(f32[2,8,1152]{2,1,0:T(8,128)S(1)} %get-tuple-element.25), channel_id=1, source_target_pairs={{0,4},{1,5},{2,6},{3,7},{4,0},{5,1},{6,2},{7,3},{8,12},{9,13},{10,... | collective-permute-start | bytes 221192 | tf_op jit(solution)/shard_map/ppermute | solution.py:275
  25.4 0.7 copy-start.4
  26.1 53.7 %copy-start = (f32[2,1024]{1,0:T(2,128)S(1)}, f32[2,1024]{1,0:T(2,128)}, u32[]{:S(2)}) copy-start(f32[2,1024]{1,0:T(2,128)} %cur_ref.1) | copy-start | bytes 24580
  26.1 53.7 %copy-start.1 = (s32[1024]{0:T(1024)S(1)}, s32[1024]{0:T(1024)}, u32[]{:S(2)}) copy-start(s32[1024]{0:T(1024)} %param.13) | copy-start | bytes 12292
  26.1 53.7 %copy-start.2 = (f32[1024]{0:T(1024)S(1)}, f32[1024]{0:T(1024)}, u32[]{:S(2)}) copy-start(f32[1024]{0:T(1024)} %param.12) | copy-start | bytes 12292
  31.4 0.8 %copy-start.3 = (f32[16,8,1152]{2,1,0:T(8,128)}, f32[16,8,1152]{2,1,0:T(8,128)S(1)}, u32[]{:S(2)}) copy-start(f32[16,8,1152]{2,1,0:T(8,128)S(1)} %all-to-all-done.col_ref) | copy-start | bytes 1769476
  60.5 3.9 %collective-permute-start.4 = (f32[2,2,1024]{2,1,0:T(2,128)}, f32[2,2,1024]{2,1,0:T(2,128)S(1)}, u32[]{:S(2)}, u32[]{:S(2)}) collective-permute-start(f32[2,2,1024]{2,1,0:T(2,128)} %get-tuple-element.18), channel_id=1, source_target_pairs={{0,2},{1,3},{2,0},{3,1},{4,6},{5,7},{6,4},{7,5},{8,10},{9,11},{10,... | collective-permute-start | bytes 49160 | tf_op jit(solution)/shard_map/ppermute | solution.py:275
  60.5 7.7 %collective-permute-start.5 = (f32[2,2,1024]{2,1,0:T(2,128)}, f32[2,2,1024]{2,1,0:T(2,128)S(1)}, u32[]{:S(2)}, u32[]{:S(2)}) collective-permute-start(f32[2,2,1024]{2,1,0:T(2,128)} %get-tuple-element.19), channel_id=1, source_target_pairs={{0,4},{1,5},{2,6},{3,7},{4,0},{5,1},{6,2},{7,3},{8,12},{9,13},{10,... | collective-permute-start | bytes 49160 | tf_op jit(solution)/shard_map/ppermute | solution.py:275
  60.6 7.6 %collective-permute-start.6 = (f32[2,2,1024]{2,1,0:T(2,128)}, f32[2,2,1024]{2,1,0:T(2,128)S(1)}, u32[]{:S(2)}, u32[]{:S(2)}) collective-permute-start(f32[2,2,1024]{2,1,0:T(2,128)} %get-tuple-element.20), channel_id=1, source_target_pairs={{0,6},{1,7},{2,4},{3,5},{4,2},{5,3},{6,0},{7,1},{8,14},{9,15},{10,... | collective-permute-start | bytes 49160 | tf_op jit(solution)/shard_map/ppermute | solution.py:275
  64.4 4.6 %collective-permute-start.8 = (f32[4,2,1024]{2,1,0:T(2,128)}, f32[4,2,1024]{2,1,0:T(2,128)S(1)}, u32[]{:S(2)}, u32[]{:S(2)}) collective-permute-start(f32[4,2,1024]{2,1,0:T(2,128)} %get-tuple-element.22), channel_id=1, source_target_pairs={{0,16},{8,24},{16,0},{24,8},{32,48},{40,56},{48,32},{56,40},{64,80... | collective-permute-start | bytes 98312 | tf_op jit(solution)/shard_map/ppermute | solution.py:275
  64.4 4.6 %collective-permute-start.9 = (f32[4,2,1024]{2,1,0:T(2,128)}, f32[4,2,1024]{2,1,0:T(2,128)S(1)}, u32[]{:S(2)}, u32[]{:S(2)}) collective-permute-start(f32[4,2,1024]{2,1,0:T(2,128)} %get-tuple-element.23), channel_id=1, source_target_pairs={{0,32},{8,40},{16,48},{24,56},{32,0},{40,8},{48,16},{56,24},{64,96... | collective-permute-start | bytes 98312 | tf_op jit(solution)/shard_map/ppermute | solution.py:275
  64.4 5.4 %collective-permute-start.10 = (f32[4,2,1024]{2,1,0:T(2,128)}, f32[4,2,1024]{2,1,0:T(2,128)S(1)}, u32[]{:S(2)}, u32[]{:S(2)}) collective-permute-start(f32[4,2,1024]{2,1,0:T(2,128)} %get-tuple-element.24), channel_id=1, source_target_pairs={{0,48},{8,56},{16,32},{24,40},{32,16},{40,24},{48,0},{56,8},{64,11... | collective-permute-start | bytes 98312 | tf_op jit(solution)/shard_map/ppermute | solution.py:275
  70.6 3.0 %collective-permute-start.11 = (f32[2,2,1024]{2,1,0:T(2,128)S(1)}, f32[2,2,1024]{2,1,0:T(2,128)S(1)}, u32[]{:S(2)}, u32[]{:S(2)}) collective-permute-start(f32[2,2,1024]{2,1,0:T(2,128)S(1)} %slice.27), channel_id=1, source_target_pairs={{0,64},{8,72},{16,80},{24,88},{32,96},{40,104},{48,112},{56,120},{... | collective-permute-start | bytes 49160 | tf_op jit(solution)/shard_map/ppermute | solution.py:275
  70.7 8.3 %collective-permute-start.7 = (f32[1,2,1024]{2,1,0:T(2,128)S(1)}, f32[1,2,1024]{2,1,0:T(2,128)S(1)}, u32[]{:S(2)}, u32[]{:S(2)}) collective-permute-start(f32[1,2,1024]{2,1,0:T(2,128)S(1)} %get-tuple-element.31), channel_id=1, source_target_pairs={{0,1},{1,0},{2,3},{3,2},{4,5},{5,4},{6,7},{7,6},{8,9},{9,8},{10,11... | collective-permute-start | bytes 24584 | tf_op jit(solution)/shard_map/ppermute | solution.py:275
  73.5 6.3 %collective-permute-start.12 = (f32[1,2,1024]{2,1,0:T(2,128)S(1)}, f32[1,2,1024]{2,1,0:T(2,128)S(1)}, u32[]{:S(2)}, u32[]{:S(2)}) collective-permute-start(f32[1,2,1024]{2,1,0:T(2,128)S(1)} %get-tuple-element.29), channel_id=1, source_target_pairs={{0,8},{8,0},{16,24},{24,16},{32,40},{40,32},{48,56},{56,48},{64,72... | collective-permute-start | bytes 24584 | tf_op jit(solution)/shard_map/ppermute | solution.py:275
